TPU v7x, 256 devices: a whole 4x4x8 slice. The times are simulated.
256 devices in a mesh: dp: 32 (over z, y), tensor: 8 (over x, core).
Axes of the slice: x: 4, y: 4, z: 8, core: 2. Of those that a mesh axis runs over, the one named last changes fastest.
Arguments:
- queries: bfloat16 [16384, 8192], P('dp', 'tensor'), may hold values from -200 to 200
- keys: bfloat16 [16384, 1024], P('dp', 'tensor'), may hold values from -6 to 6
- values: bfloat16 [16384, 1024], P('dp', 'tensor'), may hold values from -6 to 6
- outputs: bfloat16 [16384, 8192], P('dp', 'tensor'), may hold values from -2 to 2
- out_grad: bfloat16 [16384, 8192], P('dp', 'tensor'), may hold values from -24 to 24
- prefix_key: bfloat16 [8, 256, 128], P('tensor'), may hold values from -6 to 6
- prefix_value: bfloat16 [8, 256, 128], P('tensor'), may hold values from -6 to 6
- w_query: bfloat16 [8192, 8192], P('dp', 'tensor'), may hold values from -0.0625 to 0.0625
- w_key: bfloat16 [8192, 1024], P('dp', 'tensor'), may hold values from -0.1875 to 0.1875
- w_value: bfloat16 [8192, 1024], P('dp', 'tensor'), may hold values from -0.1875 to 0.1875
Outputs:
- input_grad: bfloat16 [16384, 8192], P('dp', 'tensor')
- prefix_key_grad: float32 [8, 256, 128], P('tensor')
- prefix_value_grad: float32 [8, 256, 128], P('tensor')
All inputs are finite; a program needn't handle non-finite values.
Results may differ from a plain program's by a relative error of at most 0.02.
Values may be sent and summed in bfloat16 or wider, within the bound.
No kernel may reach another device: no remote copies, remote signals or barrier semaphores. Data moves between devices by JAX's collectives and lax.ppermute only.
A program may use at most 128 MiB of HBM per device.

v0:
```python
import math

import jax
import jax.numpy as jnp
from jax import lax
from jax.sharding import PartitionSpec as P

HQ = 64
KVH = 8
LEN = 256


def attend_block(query_blk, key_blk, value_blk, output_blk, grad_blk, prefix_key, prefix_value):
    kv_local, prefix_len, head_dim = prefix_key.shape
    count = query_blk.shape[0]
    length = query_blk.shape[1]
    scale = 1.0 / math.sqrt(head_dim)
    shape_prefix = (count, prefix_len, kv_local, head_dim)
    prefix_keys = jnp.broadcast_to(jnp.transpose(prefix_key, (1, 0, 2))[None], shape_prefix)
    prefix_values = jnp.broadcast_to(jnp.transpose(prefix_value, (1, 0, 2))[None], shape_prefix)
    keyset = jnp.concatenate([prefix_keys, key_blk], axis=1)
    valueset = jnp.concatenate([prefix_values, value_blk], axis=1)
    scores = (
        jnp.einsum("rtkgd,rskd->rkgts", query_blk, keyset, preferred_element_type=jnp.float32)
        * scale
    )
    column = jnp.arange(prefix_len + length)[None, :]
    row_pos = jnp.arange(length)[:, None]
    allowed = (column < prefix_len) | (column - prefix_len <= row_pos)
    scores = jnp.where(allowed, scores, -jnp.inf)
    highest = jnp.max(scores, axis=-1, keepdims=True)
    expo = jnp.exp(scores - highest)
    probs = expo / jnp.sum(expo, axis=-1, keepdims=True)
    probs_b = probs.astype(jnp.bfloat16)
    delta = jnp.einsum(
        "rtkgd,rtkgd->rkgt", grad_blk, output_blk, preferred_element_type=jnp.float32
    )
    dprob = jnp.einsum("rtkgd,rskd->rkgts", grad_blk, valueset, preferred_element_type=jnp.float32)
    dscore_b = (probs * (dprob - delta[..., None])).astype(jnp.bfloat16)
    query_grad = (
        jnp.einsum("rkgts,rskd->rtkgd", dscore_b, keyset, preferred_element_type=jnp.float32)
        * scale
    ).astype(jnp.bfloat16)
    keyset_grad = (
        jnp.einsum("rkgts,rtkgd->rskd", dscore_b, query_blk, preferred_element_type=jnp.float32)
        * scale
    )
    valueset_grad = jnp.einsum(
        "rkgts,rtkgd->rskd", probs_b, grad_blk, preferred_element_type=jnp.float32
    )
    return (
        query_grad,
        keyset_grad[:, prefix_len:].astype(jnp.bfloat16),
        valueset_grad[:, prefix_len:].astype(jnp.bfloat16),
        jnp.sum(keyset_grad[:, :prefix_len], axis=0),
        jnp.sum(valueset_grad[:, :prefix_len], axis=0),
    )


def shards(
    queries, keys, values, outputs, out_grad, prefix_key, prefix_value, w_query, w_key, w_value
):
    kv_local, prefix_len, head_dim = prefix_key.shape
    tokens_dev = queries.shape[0]
    requests = tokens_dev // LEN
    group = HQ // KVH
    shape_five = (requests, LEN, kv_local, group, head_dim)
    shape_four = (requests, LEN, kv_local, head_dim)
    stacked = (
        queries.reshape(shape_five),
        keys.reshape(shape_four),
        values.reshape(shape_four),
        outputs.reshape(shape_five),
        out_grad.reshape(shape_five),
    )
    results = attend_block(
        stacked[0], stacked[1], stacked[2], stacked[3], stacked[4], prefix_key, prefix_value
    )
    key_total, value_total = (
        lax.psum(results[3].astype(jnp.bfloat16), "dp").astype(jnp.float32),
        lax.psum(results[4].astype(jnp.bfloat16), "dp").astype(jnp.float32),
    )
    query_grad, key_grad, value_grad = (results[0], results[1], results[2])
    grad_cat = jnp.concatenate(
        [
            query_grad.reshape(tokens_dev, -1),
            key_grad.reshape(tokens_dev, -1),
            value_grad.reshape(tokens_dev, -1),
        ],
        axis=1,
    )
    weight_cat = jnp.concatenate([w_query, w_key, w_value], axis=1)
    partial_grad = lax.dot_general(
        grad_cat,
        lax.all_gather(weight_cat, "dp", axis=0, tiled=True),
        (((1,), (1,)), ((), ())),
        preferred_element_type=jnp.float32,
    )
    input_grad = lax.psum_scatter(
        partial_grad.astype(jnp.bfloat16), "tensor", scatter_dimension=1, tiled=True
    )
    return (input_grad, jnp.transpose(key_total, (1, 0, 2)), jnp.transpose(value_total, (1, 0, 2)))


def solution(mesh):
    return jax.shard_map(
        shards,
        mesh=mesh,
        in_specs=(
            P("dp", "tensor"),
            P("dp", "tensor"),
            P("dp", "tensor"),
            P("dp", "tensor"),
            P("dp", "tensor"),
            P("tensor", None, None),
            P("tensor", None, None),
            P("dp", "tensor"),
            P("dp", "tensor"),
            P("dp", "tensor"),
        ),
        out_specs=(P("dp", "tensor"), P("tensor", None, None), P("tensor", None, None)),
        check_vma=False,
    )
```

profile of v0, /device:TPU:1, one launch (start us, length us, event | category | flops | bytes accessed | tf_op | source)
XLA Modules:
  0.0 381.3 jit_solution(5503525869861597687)
XLA Ops:
  7.2 0.0 copy-start.2
  7.2 0.0 copy-start.1
  7.2 0.0 all-gather.2.cloned.1.call-start
  7.2 2.0 pad_maximum_fusion
  9.3 0.0 all-gather.2.cloned.1.call-update
  9.3 0.0 all-reduce.3.cloned.1.call-start
  9.3 1.5 copy.42
  10.8 1.5 copy.43
  12.3 1.5 copy.44
  13.8 0.6 fusion.10
  14.5 0.1 copy.34
  14.6 0.2 fusion.27
  14.8 0.0 copy-done.2
  14.8 0.0 copy-done.1
  14.9 0.0 copy-start.3
  14.9 0.0 copy-start.4
  14.9 1.3 fusion.4
  16.2 1.7 fusion.3
  17.9 0.0 copy-done.3
  17.9 0.0 copy-done.4
  18.0 3.1 fusion.5
  21.1 0.0 copy-start
  21.1 1.2 fusion.21
  22.4 0.7 slice_reduce_fusion.1
  23.1 2.2 fusion.17
  25.4 0.0 copy-done
  25.4 0.6 slice_reduce_fusion
  26.0 0.0 all-reduce.3.cloned.1.call-update
  26.0 0.2 reduce-scatter.2.cloned.1.call-start
  26.3 3.3 fusion.11
  29.7 0.8 copy.23
  30.4 0.3 copy.57
  30.7 145.4 %all-gather.2.cloned.1.call-done = bf16[8192,1280]{1,0:T(8,128)(2,1)} async-done(((bf16[256,1280]{1,0:T(8,128)(2,1)}), bf16[8192,1280]{1,0:T(8,128)(2,1)}) %all-gather.2.cloned.1.call-update) | async-done | bytes 20971536 | tf_op jit(solution)/shard_map/all_gather | solution.py:95
  176.1 17.2 %convolution_convert_fusion = bf16[512,8192]{1,0:T(8,128)(2,1)} fusion(bf16[8192,1280]{1,0:T(8,128)(2,1)} %all-gather.2.cloned.1.call-done, bf16[512,128]{1,0:T(8,128)(2,1)S(1)} %bitcast.137, bf16[512,128]{1,0:T(8,128)(2,1)S(1)} %bitcast.136, bf16[512,1024]{1,0:T(8,128)(2,1)S(1)} %bitcast.131), kind=kOutput, calls=%fused_computation | convolution fusion | flops 10745544704 | bytes 30670848 | tf_op jit(solution)/shard_map/dot_general | solution.py:93
  193.3 0.0 reduce-scatter.2.cloned.1.call-update
  193.4 120.8 %all-reduce.3.cloned.1.call-done = (bf16[1,256,128]{2,1,0:T(8,128)(2,1)}, bf16[1,256,128]{2,1,0:T(8,128)(2,1)}) async-done(((bf16[1,256,128]{2,1,0:T(8,128)(2,1)}, bf16[1,256,128]{2,1,0:T(8,128)(2,1)}), (bf16[1,256,128]{2,1,0:T(8,128)(2,1)}, bf16[1,256,128]{2,1,0:T(8,128)(2,1)})) %all-reduce.3.cloned.1.call-update) | async-done | bytes 131088 | tf_op jit(solution)/shard_map/psum | solution.py:80
  314.2 1.5 transpose.53
  315.7 1.5 transpose.55
  317.2 57.6 %reduce-scatter.2.cloned.1.call-done = bf16[512,1024]{1,0:T(8,128)(2,1)} async-done(((bf16[512,8192]{1,0:T(8,128)(2,1)}), bf16[512,1024]{1,0:T(8,128)(2,1)}) %reduce-scatter.2.cloned.1.call-update) | async-done | bytes 1048592 | tf_op jit(solution)/shard_map/reduce_scatter | solution.py:99
  (6 shorter events, 0.1 us)
Async XLA Ops:
  7.2 7.7 %copy-start.2 = (bf16[1,256,128]{2,1,0:T(8,128)(2,1)S(1)}, bf16[1,256,128]{2,1,0:T(8,128)(2,1)}, u32[]{:S(2)}) copy-start(bf16[1,256,128]{2,1,0:T(8,128)(2,1)} %param.15) | copy-start | bytes 196612
  7.2 7.7 %copy-start.1 = (bf16[512,128]{1,0:T(8,128)(2,1)S(1)}, bf16[512,128]{1,0:T(8,128)(2,1)}, u32[]{:S(2)}) copy-start(bf16[512,128]{1,0:T(8,128)(2,1)} %param.11) | copy-start | bytes 393220
  7.2 168.9 %all-gather.2.cloned.1.call-start = ((), (), s32[]{:S(2)}) async-start(), calls=%async_computation.1 | async-start | bytes 21626880 | tf_op jit(solution)/shard_map/all_gather | solution.py:95
  9.3 304.9 %all-reduce.3.cloned.1.call-start = ((), (), s32[]{:S(2)}) async-start(), calls=%async_computation.3 | async-start | bytes 262144 | tf_op jit(solution)/shard_map/psum | solution.py:80
  14.9 3.1 copy-start.3
  14.9 3.1 copy-start.4
  21.1 4.3 %copy-start = (bf16[2,8,256,512]{2,3,1,0:T(8,128)(2,1)}, bf16[2,8,256,512]{2,3,1,0:T(8,128)(2,1)S(1)}, u32[]{:S(2)}) copy-start(bf16[2,8,256,512]{2,3,1,0:T(8,128)(2,1)S(1)} %fusion.5) | copy-start | bytes 12582916
  26.0 348.8 %reduce-scatter.2.cloned.1.call-start = ((), (), s32[]{:S(2)}) async-start(), calls=%async_computation.2 | async-start | bytes 9437184 | tf_op jit(solution)/shard_map/reduce_scatter | solution.py:99
Sparse Core Ops, SparseCore 0:
  11.2 164.8 all-gather.1
  180.2 133.9 all-reduce.2
  317.5 57.3 reduce-scatter.1
where the time goes:
time: 382 us; the launch traced here: 381 us
  waiting for transfers between devices  324 us (85%)
  matrix products  28.5 us (7%)
  between operations  14 us (4%)
  other arithmetic  8.99 us (2%)
  local copies, waits for them, and re-layouts  5.68 us (1%)
    all_gather x1, waiting for transfers between devices, shards(): lax.all_gather(weight_cat, 'dp', axis=0, tiled=True)  145 us
    psum x1, waiting for transfers between devices, shards(): lax.psum(results[3].astype(jnp.bfloat16), 'dp').astype(jnp.float32)  121 us
    reduce_scatter x1, waiting for transfers between devices, shards(): lax.psum_scatter(partial_grad.astype(jnp.bfloat16), 'tensor', scatter_dim...  57.6 us
    dot_general x1, matrix products, shards(): lax.dot_general(grad_cat, lax.all_gather(weight_cat, 'dp', axis=0, tiled=...  17.2 us
  transfers between devices with their start and end apart: 3, of which 3 were waited for; matrix products, arithmetic and copies ran while one was open for 11% of the time, Pallas kernels for 0%

commit v1 on v0

v1 whole, which is shorter than its diff:
```python
import math

import jax
import jax.numpy as jnp
from jax import lax
from jax.experimental import pallas as pl
from jax.experimental.pallas import tpu as pltpu
from jax.sharding import Mesh
from jax.sharding import PartitionSpec as P

LEN = 256
HEADS = 8
HD = 128
NZ, NY, NX, NC = 8, 4, 4, 2
MIB = 1024 * 1024
VMEM_SMALL = 16 * MIB
VMEM_PRODUCT = 24 * MIB
SMALL = pl.CostEstimate(flops=1024, bytes_accessed=1024, transcendentals=0)
NT_DIMS = (((1,), (1,)), ((), ()))


def attend_kernel(
    q_ref, k_ref, v_ref, o_ref, g_ref, pk_ref, pv_ref, grad_ref, sum_ref, pre_ref, keyset, valueset, dk_acc, dv_acc
):
    req = pl.program_id(0)
    prefix = pk_ref.shape[1]
    rows = pl.ds(pl.multiple_of(req * LEN, LEN), LEN)
    scale = 1.0 / math.sqrt(HD)
    unit = scale * math.log2(math.e)
    keyset[:prefix] = pk_ref[0]
    keyset[prefix:] = k_ref[...]
    valueset[:prefix] = pv_ref[0]
    valueset[prefix:] = v_ref[...]
    lane = lax.broadcasted_iota(jnp.int32, (LEN, HD), 1)
    spread = jnp.zeros((LEN, HD), jnp.float32)
    for h in range(HEADS):
        cols = pl.ds(h * HD, HD)
        delta = jnp.sum(
            g_ref[:, cols].astype(jnp.float32) * o_ref[:, cols].astype(jnp.float32),
            axis=1,
            keepdims=True,
        )
        spread = jnp.where(lane == h, delta, spread)
    deltas = spread.T
    key_pos = lax.broadcasted_iota(jnp.int32, (LEN, LEN), 0)
    tok_pos = lax.broadcasted_iota(jnp.int32, (LEN, LEN), 1)
    seen = key_pos <= tok_pos
    keys = keyset[...]
    vals = valueset[...]
    for h in range(HEADS):
        cols = pl.ds(h * HD, HD)
        q = q_ref[:, cols]
        g = g_ref[:, cols]
        s = lax.dot_general(keys, q, NT_DIMS, preferred_element_type=jnp.float32)
        s_a = s[:prefix]
        s_b = jnp.where(seen, s[prefix:], -jnp.inf)
        top = jnp.maximum(
            jnp.max(s_a, axis=0, keepdims=True), jnp.max(s_b, axis=0, keepdims=True)
        )
        e_a = jnp.exp2((s_a - top) * unit)
        e_b = jnp.exp2((s_b - top) * unit)
        total = jnp.sum(e_a, axis=0, keepdims=True) + jnp.sum(e_b, axis=0, keepdims=True)
        inv = 1.0 / total
        probs = jnp.concatenate([e_a * inv, e_b * inv], axis=0)
        dprob = lax.dot_general(vals, g, NT_DIMS, preferred_element_type=jnp.float32)
        dscore = (probs * (dprob - deltas[h : h + 1, :])).astype(jnp.bfloat16)
        probs_b = probs.astype(jnp.bfloat16)
        dq = lax.dot_general(
            dscore, keys, (((0,), (0,)), ((), ())), preferred_element_type=jnp.float32
        )
        grad_ref[rows, cols] = (dq * scale).astype(jnp.bfloat16)
        dk = jnp.dot(dscore, q, preferred_element_type=jnp.float32)
        dv = jnp.dot(probs_b, g, preferred_element_type=jnp.float32)
        if h == 0:
            dk_acc[...] = dk
            dv_acc[...] = dv
        else:
            dk_acc[...] += dk
            dv_acc[...] += dv
    width = HEADS * HD
    grad_ref[rows, pl.ds(width, HD)] = (dk_acc[prefix:] * scale).astype(jnp.bfloat16)
    grad_ref[rows, pl.ds(width + HD, HD)] = dv_acc[prefix:].astype(jnp.bfloat16)

    @pl.when(req == 0)
    def _():
        pre_ref[:prefix] = dk_acc[:prefix] * scale
        pre_ref[prefix:] = dv_acc[:prefix]

    @pl.when(req == pl.num_programs(0) - 1)
    def _():
        pre_ref[:prefix] += dk_acc[:prefix] * scale
        pre_ref[prefix:] += dv_acc[:prefix]
        sum_ref[...] = pre_ref[...].astype(jnp.bfloat16)


def attend(q, k, v, o, g, pk, pv):
    prefix = pk.shape[1]
    tokens, width = q.shape
    wide = pl.BlockSpec((LEN, width), lambda i: (i, 0))
    slim = pl.BlockSpec((LEN, HD), lambda i: (i, 0))
    pre = pl.BlockSpec((1, prefix, HD), lambda i: (0, 0, 0))
    return pl.pallas_call(
        attend_kernel,
        grid=(tokens // LEN,),
        in_specs=[wide, slim, slim, wide, wide, pre, pre],
        out_specs=[
            pl.BlockSpec((tokens, width + 2 * HD), lambda i: (0, 0)),
            pl.BlockSpec((2 * prefix, HD), lambda i: (0, 0)),
        ],
        out_shape=[
            jax.ShapeDtypeStruct((tokens, width + 2 * HD), jnp.bfloat16),
            jax.ShapeDtypeStruct((2 * prefix, HD), jnp.bfloat16),
        ],
        scratch_shapes=[pltpu.VMEM((2 * prefix, HD), jnp.float32)]
        + [pltpu.VMEM((prefix + LEN, HD), jnp.bfloat16)] * 2
        + [pltpu.VMEM((prefix + LEN, HD), jnp.float32)] * 2,
        compiler_params=pltpu.CompilerParams(vmem_limit_bytes=56 * MIB),
        cost_estimate=SMALL,
    )(q, k, v, o, g, pk, pv)


def product_kernel(offsets, counts, sizes, phases, base, extra, *refs):
    z, x, c = lax.axis_index("z"), lax.axis_index("x"), lax.axis_index("c")
    parts = refs[: sum(counts)]
    rest = refs[sum(counts) :]
    grads = rest[: len(sizes)]
    rest = rest[len(sizes) + extra :]
    outs = rest[:8]
    stamp, wbuf, gbuf, wsem, gsem, osem = rest[8:14]
    obufs = rest[14:]
    stamp[...] = jnp.zeros_like(stamp)
    width = wbuf.shape[0] // len(counts)

    def w_wait(tile):
        where = wbuf.at[pl.ds(pl.multiple_of(tile * width, width), width)]
        pltpu.make_async_copy(where, where, wsem.at[tile]).wait()

    w_copies = []
    at = 0
    for tile, count in enumerate(counts):
        row = tile * width
        w_copies.append([])
        for _ in range(count):
            src = parts[at]
            dst = wbuf.at[pl.ds(row, src.shape[0])]
            w_copies[-1].append(pltpu.make_async_copy(src, dst, wsem.at[tile]))
            row += src.shape[0]
            at += 1
    g_copies = []
    row = 0
    for blk, size in enumerate(sizes):
        src = grads[blk].at[:, pl.ds(0, gbuf.shape[1])]
        g_copies.append(pltpu.make_async_copy(src, gbuf.at[pl.ds(row, size)], gsem.at[blk]))
        row += size

    def blocks_of(phase):
        at = 0
        for blk, size in enumerate(sizes):
            if at < phase[3] + phase[4] and at + size > phase[3]:
                yield blk
            at += size

    def tiles_of(phase):
        return range(phase[0], phase[0] + phase[1] * phase[2])

    started = set()
    for phase in phases:
        for blk in blocks_of(phase):
            if blk not in started:
                g_copies[blk].start()
                started.add(blk)
        for tile in tiles_of(phase):
            if -1 - tile not in started:
                for copy in w_copies[tile]:
                    copy.start()
                started.add(-1 - tile)

    ended = set()
    drains = []
    for which, phase in enumerate(phases):
        tile_0, groups, per, first, rows = phase
        for blk in blocks_of(phase):
            if blk not in ended:
                g_copies[blk].wait()
                ended.add(blk)
        fresh = -1 - tile_0 not in ended
        for tile in tiles_of(phase):
            ended.add(-1 - tile)
        obuf = obufs[which]
        where = pl.ds(base + first, rows)

        def copy_out(slot, k, value, obuf=obuf, where=where, which=which):
            return pltpu.make_async_copy(
                obuf.at[slot, :, pl.ds(k * width, width)], outs[value].at[where], osem.at[which, slot, k]
            )

        def one(i):
            slot = lax.rem(i, 2)

            @pl.when(i >= 2)
            def _():
                for k in range(per):
                    copy_out(slot, k, 0).wait()

            if fresh:
                for k in range(per):
                    w_wait(tile_0 + i * per + k)
            start = pl.multiple_of((tile_0 + i * per) * width, width)
            obuf[slot] = lax.dot_general(
                gbuf[pl.ds(first, rows), :],
                wbuf[pl.ds(start, per * width), :],
                NT_DIMS,
                preferred_element_type=jnp.float32,
            ).astype(jnp.bfloat16)
            for k in range(per):
                tile = tile_0 + i * per + k
                off = jnp.int32(offsets[0])
                for t in range(1, len(offsets)):
                    off = jnp.where(tile == t, jnp.int32(offsets[t]), off)
                row = lax.rem(z + off, NZ)
                rel = lax.rem(lax.div(row, 2) - x + NX, NX)
                place = rel + jnp.where(lax.rem(row, 2) == c, 4, 0)
                for value in range(8):
                    @pl.when(place == value)
                    def _():
                        copy_out(slot, k, value).start()

        pl.loop(0, groups)(one)
        drains += [(copy_out, slot, k) for slot in range(min(2, groups)) for k in range(per)]
    for copy_out, slot, k in drains:
        copy_out(slot, k, 0).wait()


def product(offsets, tiles, grads, phases, base, total, prev=None, deps=()):
    counts = [len(tile) for tile in tiles]
    flat = [part for tile in tiles for part in tile]
    rows = sum(part.shape[0] for part in tiles[0])
    depth = flat[0].shape[1]
    sizes = [g.shape[0] for g in grads]
    anywhere = pl.BlockSpec(memory_space=pl.ANY)
    hbm = pl.BlockSpec(memory_space=pltpu.HBM)
    args = [*flat, *grads]
    given = len(args)
    aliases = {}
    if prev is not None:
        aliases = {len(args) + i: i for i in range(8)}
        args += list(prev)
    args += list(deps)
    extra = len(args) - len(flat) - len(grads)

    def body(*refs):
        product_kernel(offsets, counts, sizes, phases, base, extra, *refs)

    results = pl.pallas_call(
        body,
        in_specs=[hbm] * given + [anywhere] * (len(args) - given),
        out_specs=[anywhere] * 8 + [pl.BlockSpec(memory_space=pltpu.VMEM)],
        out_shape=[jax.ShapeDtypeStruct((total, rows), jnp.bfloat16)] * 8
        + [jax.ShapeDtypeStruct((8, 128), jnp.float32)],
        input_output_aliases=aliases,
        scratch_shapes=[
            pltpu.VMEM((len(tiles) * rows, depth), jnp.bfloat16),
            pltpu.VMEM((sum(sizes), depth), jnp.bfloat16),
            pltpu.SemaphoreType.DMA((len(tiles),)),
            pltpu.SemaphoreType.DMA((len(grads),)),
            pltpu.SemaphoreType.DMA((len(phases), 2, max(phase[2] for phase in phases))),
        ]
        + [pltpu.VMEM((2, phase[4], phase[2] * rows), jnp.bfloat16) for phase in phases],
        compiler_params=pltpu.CompilerParams(vmem_limit_bytes=VMEM_PRODUCT),
        cost_estimate=SMALL,
    )(*args)
    return results[:-1], results[-1]


def pack_kernel(a_ref, b_ref, c_ref, out_ref):
    at = 0
    for ref in (a_ref, b_ref, c_ref):
        out_ref[:, pl.ds(at, ref.shape[1])] = ref[...]
        at += ref.shape[1]


def pack(*parts):
    width = sum(part.shape[1] for part in parts)
    return pl.pallas_call(
        pack_kernel,
        out_shape=jax.ShapeDtypeStruct((parts[0].shape[0], width), parts[0].dtype),
        compiler_params=pltpu.CompilerParams(vmem_limit_bytes=56 * MIB),
        cost_estimate=SMALL,
    )(*parts)


def lay_kernel(*refs):
    y = lax.axis_index("y")
    out_ref = refs[NY]
    for i, ref in enumerate(refs[:NY]):
        width = ref.shape[1]
        start = pl.multiple_of(lax.rem(y + i, NY) * width, width)
        out_ref[:, pl.ds(start, width)] = ref[...]


def lay(pieces):
    rows, width = pieces[0].shape
    whole = pl.BlockSpec((rows, width), lambda: (0, 0))
    return pl.pallas_call(
        lay_kernel,
        in_specs=[whole] * NY,
        out_shape=jax.ShapeDtypeStruct((rows, NY * width), pieces[0].dtype),
        compiler_params=pltpu.CompilerParams(vmem_limit_bytes=VMEM_SMALL),
        cost_estimate=SMALL,
    )(*pieces)


def cut_kernel(*refs):
    for src, dst in zip(refs[:4], refs[4:], strict=True):
        dst[...] = src[...]


def cut(*pairs):
    arrays = [array for pair in pairs for array in pair]

    def spec(array, at):
        return pl.BlockSpec((array.shape[0] // 2, array.shape[1]), lambda i: (at, 0))

    return pl.pallas_call(
        cut_kernel,
        grid=(1,),
        in_specs=[spec(array, i % 2) for i, array in enumerate(arrays)],
        out_specs=[spec(array, 0) for array in arrays],
        out_shape=[
            jax.ShapeDtypeStruct((a.shape[0] // 2, a.shape[1]), a.dtype) for a in arrays
        ],
        compiler_params=pltpu.CompilerParams(vmem_limit_bytes=VMEM_SMALL),
        cost_estimate=SMALL,
    )(*arrays)


def add_refs(*refs):
    total = refs[0].astype(jnp.float32)
    for ref in refs[1:]:
        total = total + ref.astype(jnp.float32)
    return total.astype(jnp.bfloat16)


def by_rows(kernel, rows, first, tokens, args, widths, deps=()):
    def spec(array):
        skip = first // rows if array.shape[0] > tokens else 0
        return pl.BlockSpec((rows, array.shape[1]), lambda i: (i + skip, 0))

    shapes = [jax.ShapeDtypeStruct((tokens, width), jnp.bfloat16) for width in widths]
    return pl.pallas_call(
        kernel,
        grid=(tokens // rows,),
        in_specs=[spec(arg) for arg in args] + [pl.BlockSpec(memory_space=pl.ANY)] * len(deps),
        out_specs=[spec(shape) for shape in shapes],
        out_shape=shapes,
        compiler_params=pltpu.CompilerParams(vmem_limit_bytes=VMEM_SMALL),
        cost_estimate=SMALL,
    )(*args, *deps)


def far_kernel(keep, got, *refs):
    a_ref, b_ref = refs[-2:]
    half = a_ref.shape[1]
    a_ref[...] = add_refs(keep[:, :half], got[:, :half])
    b_ref[...] = add_refs(keep[:, half:], got[:, half:])


def near_kernel(keep_up, got_up, far_up, keep_down, got_down, far_down, *refs):
    up, down = refs[-2:]
    half = far_up.shape[1]
    up[:, :half] = add_refs(keep_up[:, :half], got_up[:, :half], far_up[...])
    up[:, half:] = add_refs(keep_up[:, half:], got_up[:, half:])
    down[:, :half] = add_refs(keep_down[:, :half], got_down[:, :half])
    down[:, half:] = add_refs(keep_down[:, half:], got_down[:, half:], far_down[...])


def total_kernel(keep, got, up, down, out):
    out[...] = add_refs(keep[...], got[...], up[...], down[...])


def total(row, row_got, rows, keep, got, up, down):
    def spec(first):
        at = first // rows
        return pl.BlockSpec((rows, keep.shape[1]), lambda i: (at, 0))

    return pl.pallas_call(
        total_kernel,
        grid=(1,),
        in_specs=[spec(row), spec(row), spec(row_got), spec(row_got)],
        out_specs=spec(0),
        out_shape=jax.ShapeDtypeStruct((rows, keep.shape[1]), jnp.bfloat16),
        compiler_params=pltpu.CompilerParams(vmem_limit_bytes=VMEM_SMALL),
        cost_estimate=SMALL,
    )(keep, got, up, down)


def prefix_kernel(own, other, *refs):
    refs[-1][...] = (own[...].astype(jnp.float32) + other[...].astype(jnp.float32)).astype(
        refs[-1].dtype
    )


def prefix_add(own, other, dtype, *deps):
    whole = pl.BlockSpec(memory_space=pltpu.VMEM)
    return pl.pallas_call(
        prefix_kernel,
        in_specs=[whole] * 2 + [pl.BlockSpec(memory_space=pl.ANY)] * len(deps),
        out_specs=whole,
        out_shape=jax.ShapeDtypeStruct(own.shape, dtype),
        compiler_params=pltpu.CompilerParams(vmem_limit_bytes=VMEM_SMALL),
        cost_estimate=SMALL,
    )(own, other, *deps)


def shift(value, axis, size, by):
    return lax.ppermute(value, axis, [(i, (i + by) % size) for i in range(size)])


def swap(value, axis, size, mask):
    return lax.ppermute(value, axis, [(i, i ^ mask) for i in range(size)])


def shards(
    queries, keys, values, outputs, out_grad, prefix_key, prefix_value, w_query, w_key, w_value
):
    tokens = queries.shape[0]
    every = NY * tokens
    weight = pack(w_query, w_key, w_value)

    tiles = {0: (weight,)}
    with jax.named_scope("weights"):
        up = down = weight
        for step in range(1, 4):
            up = shift(up, "z", NZ, 1)
            down = shift(down, "z", NZ, -1)
            tiles[NZ - step], tiles[step] = (up,), (down,)

    grad, prefix_sum = attend(
        queries, keys, values, outputs, out_grad, prefix_key, prefix_value
    )
    with jax.named_scope("grads"):
        g_up = shift(grad, "y", NY, 1)
        g_down = shift(grad, "y", NY, -1)
    up_half, down_half, up_tile, down_tile = cut((g_up, g_down), (up, down))
    with jax.named_scope("grads_far"):
        far_a = shift(up_half, "y", NY, 1)
        far_b = shift(down_half, "y", NY, -1)
    with jax.named_scope("weights_far"):
        tiles[4] = (shift(up_tile, "z", NZ, 1), shift(down_tile, "z", NZ, -1))

    near = [g_up, grad, g_down]
    rest = every - tokens
    offsets = [0, 1, 7, 2, 6, 3, 5, 4]
    part, stamp = product(
        offsets[:7],
        [tiles[off] for off in offsets[:7]],
        near,
        [(0, 3, 2, 0, rest), (6, 1, 1, 0, rest)],
        tokens,
        every,
    )
    part, _ = product(
        offsets,
        [tiles[off] for off in offsets],
        [far_a, far_b, *near],
        [(0, 2, 4, 0, tokens), (7, 1, 1, tokens, rest)],
        0,
        every,
        part,
        deps=(stamp,),
    )

    send, keep = part[:4], part[4:]
    with jax.named_scope("sum_c"):
        got = {rel: swap(send[rel], "c", NC, 1) for rel in (2, 1, 3, 0)}
    width = keep[0].shape[1]
    far_sum = by_rows(far_kernel, 2 * LEN, 0, every, [keep[2], got[2]], [width // 2] * 2)
    with jax.named_scope("sum_x1"):
        far_up = shift(far_sum[0], "x", NX, 1)
        far_down = shift(far_sum[1], "x", NX, -1)
    args = [keep[1], got[1], far_up, keep[3], got[3], far_down]
    prefix = prefix_sum
    with jax.named_scope("prefix"):
        prefix = prefix_add(prefix, swap(prefix, "z", NZ, 1), jnp.bfloat16)
        prefix = prefix_add(prefix, swap(prefix, "z", NZ, 2), jnp.bfloat16)
    dep = (prefix,)
    sums = []
    for first in (0, every // 2):
        ways = by_rows(near_kernel, 2 * LEN, first, every // 2, args, [width] * 2, dep)
        dep = (ways[0],)
        with jax.named_scope("sum_x2"):
            got_up = shift(ways[0], "x", NX, 1)
            got_down = shift(ways[1], "x", NX, -1)
        for part_first in (0, tokens):
            sums.append((first + part_first, part_first, got_up, got_down))
    blocks = []
    for row, row_got, got_up, got_down in sums:
        blocks.append(total(row, row_got, tokens, keep[0], got[0], got_up, got_down))
    from_far, from_up, own, from_down = blocks

    with jax.named_scope("prefix"):
        prefix = prefix_add(prefix, swap(prefix, "z", NZ, 4), jnp.bfloat16, *dep)
        prefix = prefix_add(prefix, swap(prefix, "y", NY, 1), jnp.bfloat16)
        prefix_total = prefix_add(prefix, swap(prefix, "y", NY, 2), jnp.float32)

    with jax.named_scope("back"):
        back_far = shift(from_far, "y", NY, 2)
        back_up = shift(from_up, "y", NY, -1)
        back_down = shift(from_down, "y", NY, 1)
    input_grad = lay([own, back_up, back_far, back_down])
    prefix_len = prefix_key.shape[1]
    return (input_grad, prefix_total[None, :prefix_len], prefix_total[None, prefix_len:])


def solution(mesh):
    fine = Mesh(mesh.devices.reshape(NZ, NY, NX, NC), ("z", "y", "x", "c"))
    full = P(("z", "y"), ("x", "c"))
    head = P(("x", "c"), None, None)
    return jax.shard_map(
        shards,
        mesh=fine,
        in_specs=(full, full, full, full, full, head, head, full, full, full),
        out_specs=(full, head, head),
        check_vma=False,
    )
```

time: 382 us -> 155 us (0.41)
  waiting for transfers between devices: 324 us -> 72.1 us
  starting transfers between devices: 0.3 us -> 41.9 us
  Pallas kernels: 0 us -> 37.4 us
  matrix products: 28.5 us -> 0 us
  between operations: 14 us -> 0.83 us
  other arithmetic: 8.99 us -> 0 us
  local copies, waits for them, and re-layouts: 5.68 us -> 0.73 us
    all_gather x1 -> x0, waiting for transfers between devices: 145 us -> none  [shards(): lax.all_gather(weight_cat, 'dp', axis=0, tiled=True)]
    psum x1 -> x0, waiting for transfers between devices: 121 us -> none  [shards(): lax.psum(results[3].astype(jnp.bfloat16), 'dp').astype(jnp.float32)]
    ppermute x0 -> x30, waiting for transfers between devices: none -> 72.1 us  [the longest x21 54 us: shift(): lax.ppermute(value, axis, [(i, (i + by) % size) for i in range(size)])]
    reduce_scatter x1 -> x0, waiting for transfers between devices: 57.6 us -> none  [shards(): lax.psum_scatter(partial_grad.astype(jnp.bfloat16), 'tensor', scatter_dim...]
    ppermute x0 -> x30, starting transfers between devices: none -> 41.9 us  [the longest x21 33.6 us: shift(): lax.ppermute(value, axis, [(i, (i + by) % size) for i in range(size)])]
    pallas_call x0 -> x18, Pallas kernels: none -> 37.4 us  [the longest x2 18.9 us: product(): pl.pallas_call(body, in_specs=[hbm] * given + [anywhere] * (len(args) - g...]
    dot_general x6 -> x0, matrix products: 28.5 us -> none  [the longest x1 17.2 us: shards(): lax.dot_general(grad_cat, lax.all_gather(weight_cat, 'dp', axis=0, tiled=...]
    unnamed x14 -> x6, local copies, waits for them, and re-layouts: 4.77 us -> 0.01 us
  transfers between devices with their start and end apart: 3 -> 30, of which waited for: 3 -> 13; matrix products, arithmetic and copies ran while one was open for 11% -> 0% of each run, Pallas kernels for 0% -> 17%
where the time goes in v1:
time: 155 us; the launch traced here: 153 us
  waiting for transfers between devices  72.1 us (47%)
  starting transfers between devices  41.9 us (27%)
  Pallas kernels  37.4 us (24%)
    ppermute x21, waiting for transfers between devices, shift(): lax.ppermute(value, axis, [(i, (i + by) % size) for i in range(size)])  54 us
    ppermute x21, starting transfers between devices, shift(): lax.ppermute(value, axis, [(i, (i + by) % size) for i in range(size)])  33.6 us
    pallas_call x2, Pallas kernels, product(): pl.pallas_call(body, in_specs=[hbm] * given + [anywhere] * (len(args) - g...  18.9 us
    ppermute x9, waiting for transfers between devices, swap(): return lax.ppermute(value, axis, [(i, i ^ mask) for i in range(size)])  18.1 us
    pallas_call x1, Pallas kernels, attend(): pl.pallas_call(attend_kernel, grid=(tokens // LEN,), in_specs=[wide, slim...  13.5 us
    ppermute x9, starting transfers between devices, swap(): return lax.ppermute(value, axis, [(i, i ^ mask) for i in range(size)])  8.29 us
  transfers between devices with their start and end apart: 30, of which 13 were waited for; matrix products, arithmetic and copies ran while one was open for 0% of the time, Pallas kernels for 17%

profile of v1, /device:TPU:1, one launch (start us, length us, event | category | flops | bytes accessed | tf_op | source)
XLA Modules:
  0.0 153.0 jit_solution(4446538824182621892)
XLA Ops:
  0.6 2.0 %shard_map.121.refs_0_ = bf16[256,1280]{1,0:T(8,128)(2,1)} custom-call(bf16[256,1024]{1,0:T(8,128)(2,1)} %a_ref.1, bf16[256,128]{1,0:T(8,128)(2,1)} %b_ref.1, bf16[256,128]{1,0:T(8,128)(2,1)} %c_ref.1), custom_call_target="tpu_custom_call" | custom-call | flops 1024 | bytes 1024 | tf_op jit(solution)/shard_map/pallas_call | solution.py:284
  2.6 6.4 %collective-permute-start = (bf16[256,1280]{1,0:T(8,128)(2,1)}, bf16[256,1280]{1,0:T(8,128)(2,1)S(1)}, u32[]{:S(2)}, u32[]{:S(2)}) collective-permute-start(bf16[256,1280]{1,0:T(8,128)(2,1)} %shard_map.121.refs_0_), channel_id=1, source_target_pairs={{0,224},{32,0},{64,32},{96,64},{128,96},{160,128},{192,160},{224,1... | collective-permute-start | bytes 1966088 | tf_op jit(solution)/shard_map/weights/ppermute | solution.py:416
  9.0 13.5 %shard_map.122 = (bf16[512,1280]{1,0:T(8,128)(2,1)}, bf16[512,128]{1,0:T(8,128)(2,1)}) custom-call(bf16[512,1024]{1,0:T(8,128)(2,1)} %q_ref.1, bf16[512,128]{1,0:T(8,128)(2,1)} %k_ref.1, bf16[512,128]{1,0:T(8,128)(2,1)} %v_ref.1, bf16[512,1024]{1,0:T(8,128)(2,1)} %o_ref.1, bf16[512,1024]{1,0:T(8,128)(2,1)} %g_ref.1, bf16[1,256,128]{2,1,0:T(8,128)(2,1)} %pk_ref.1, ...), custom_call_target="tpu_custom_call" | custom-call | flops 1024 | bytes 1024 | tf_op jit(solution)/shard_map/pallas_call | solution.py:102
  22.5 1.4 collective-permute-start.6
  23.9 1.5 collective-permute-start.7
  25.4 2.7 %collective-permute-start.2 = (bf16[256,1280]{1,0:T(8,128)(2,1)S(1)}, bf16[256,1280]{1,0:T(8,128)(2,1)S(1)}, u32[]{:S(2)}, u32[]{:S(2)}) collective-permute-start(bf16[256,1280]{1,0:T(8,128)(2,1)S(1)} %collective-permute-done.refs_1_), channel_id=1, source_target_pairs={{0,224},{32,0},{64,32},{96,64},{128,96},{160,128},{192,160},{224,1... | collective-permute-start | bytes 1966088 | tf_op jit(solution)/shard_map/weights/ppermute | solution.py:416
  28.1 12.4 %collective-permute-done.2.refs_3_ = bf16[256,1280]{1,0:T(8,128)(2,1)S(1)} collective-permute-done((bf16[256,1280]{1,0:T(8,128)(2,1)S(1)}, bf16[256,1280]{1,0:T(8,128)(2,1)S(1)}, u32[]{:S(2)}, u32[]{:S(2)}) %collective-permute-start.2) | collective-permute-done | bytes 655392 | tf_op jit(solution)/shard_map/weights/ppermute | solution.py:416
  40.5 3.4 %collective-permute-start.4 = (bf16[256,1280]{1,0:T(8,128)(2,1)S(1)}, bf16[256,1280]{1,0:T(8,128)(2,1)S(1)}, u32[]{:S(2)}, u32[]{:S(2)}) collective-permute-start(bf16[256,1280]{1,0:T(8,128)(2,1)S(1)} %collective-permute-done.2.refs_3_), channel_id=1, source_target_pairs={{0,224},{32,0},{64,32},{96,64},{128,96},{160,128},{192,160},{224,1... | collective-permute-start | bytes 1966088 | tf_op jit(solution)/shard_map/weights/ppermute | solution.py:416
  43.9 9.6 %collective-permute-done.6.refs_0_.refs_7_.refs_11_ = bf16[512,1280]{1,0:T(8,128)(2,1)S(1)} collective-permute-done((bf16[512,1280]{1,0:T(8,128)(2,1)}, bf16[512,1280]{1,0:T(8,128)(2,1)S(1)}, u32[]{:S(2)}, u32[]{:S(2)}) %collective-permute-start.6) | collective-permute-done | bytes 1310752 | tf_op jit(solution)/shard_map/grads/ppermute | solution.py:416
  53.5 1.9 %collective-permute-done.4.refs_3_.refs_5_ = bf16[256,1280]{1,0:T(8,128)(2,1)S(1)} collective-permute-done((bf16[256,1280]{1,0:T(8,128)(2,1)S(1)}, bf16[256,1280]{1,0:T(8,128)(2,1)S(1)}, u32[]{:S(2)}, u32[]{:S(2)}) %collective-permute-start.4) | collective-permute-done | bytes 655392 | tf_op jit(solution)/shard_map/weights/ppermute | solution.py:416
  55.3 3.1 %collective-permute-done.5.refs_2_.refs_6_ = bf16[256,1280]{1,0:T(8,128)(2,1)S(1)} collective-permute-done((bf16[256,1280]{1,0:T(8,128)(2,1)S(1)}, bf16[256,1280]{1,0:T(8,128)(2,1)S(1)}, u32[]{:S(2)}, u32[]{:S(2)}) %collective-permute-start.5) | collective-permute-done | bytes 655392 | tf_op jit(solution)/shard_map/weights/ppermute | solution.py:416
  58.5 0.1 shard_map.123
  58.7 2.7 %collective-permute-start.11 = (bf16[256,1280]{1,0:T(8,128)(2,1)S(1)}, bf16[256,1280]{1,0:T(8,128)(2,1)S(1)}, u32[]{:S(2)}, u32[]{:S(2)}) collective-permute-start(bf16[256,1280]{1,0:T(8,128)(2,1)S(1)} %get-tuple-element.36), channel_id=1, source_target_pairs={{0,24},{8,0},{16,8},{24,16},{1,25},{9,1},{17,9},{25,17},{2,26},{10... | collective-permute-start | bytes 1966088 | tf_op jit(solution)/shard_map/grads_far/ppermute | solution.py:416
  61.4 2.7 %collective-permute-start.9 = (bf16[128,1280]{1,0:T(8,128)(2,1)S(1)}, bf16[128,1280]{1,0:T(8,128)(2,1)S(1)}, u32[]{:S(2)}, u32[]{:S(2)}) collective-permute-start(bf16[128,1280]{1,0:T(8,128)(2,1)S(1)} %get-tuple-element.34), channel_id=1, source_target_pairs={{0,224},{32,0},{64,32},{96,64},{128,96},{160,128},{192,160},{224,1... | collective-permute-start | bytes 983048 | tf_op jit(solution)/shard_map/weights_far/ppermute | solution.py:416
  64.0 10.6 %shard_map.124 = (bf16[2048,256]{1,0:T(8,128)(2,1)S(1)}, bf16[2048,256]{1,0:T(8,128)(2,1)S(1)}, bf16[2048,256]{1,0:T(8,128)(2,1)S(1)}, bf16[2048,256]{1,0:T(8,12...) custom-call(bf16[256,1280]{1,0:T(8,128)(2,1)S(1)} %copy-done, ...), custom_call_target="tpu_custom_call" | custom-call | flops 1024 | bytes 1024 | tf_op jit(solution)/shard_map/pallas_call | solution.py:254
  74.7 8.3 %shard_map.125 = (bf16[2048,256]{1,0:T(8,128)(2,1)S(1)}, bf16[2048,256]{1,0:T(8,128)(2,1)S(1)}, bf16[2048,256]{1,0:T(8,128)(2,1)S(1)}, bf16[2048,256]{1,0:T(8,12...) custom-call(bf16[256,1280]{1,0:T(8,128)(2,1)S(1)} %copy-done, ...), custom_call_target="tpu_custom_call", output_to_operand_aliasing={{0}: (14, {}), {1}: (15, {}), {2}: (16, {}), {3}: (17, {}),... | custom-call | flops 1024 | bytes 1024 | tf_op jit(solution)/shard_map/pallas_call | solution.py:254
  83.1 5.0 %collective-permute-start.14 = (bf16[2048,256]{1,0:T(8,128)(2,1)S(1)}, bf16[2048,256]{1,0:T(8,128)(2,1)S(1)}, u32[]{:S(2)}, u32[]{:S(2)}) collective-permute-start(bf16[2048,256]{1,0:T(8,128)(2,1)S(1)} %get-tuple-element.51), channel_id=1, source_target_pairs={{0,1},{1,0},{2,3},{3,2},{4,5},{5,4},{6,7},{7,6},{8,9},{9,8},{10,11... | collective-permute-start | bytes 3145736 | tf_op jit(solution)/shard_map/sum_c/ppermute | solution.py:420
  88.1 0.4 collective-permute-start.16
  88.6 5.1 %collective-permute-done.18.other = bf16[512,128]{1,0:T(8,128)(2,1)S(1)} collective-permute-done((bf16[512,128]{1,0:T(8,128)(2,1)S(1)}, bf16[512,128]{1,0:T(8,128)(2,1)S(1)}, u32[]{:S(2)}, u32[]{:S(2)}) %collective-permute-start.18) | collective-permute-done | bytes 131104 | tf_op jit(solution)/shard_map/prefix/ppermute | solution.py:420
  93.7 0.3 collective-permute-start.19
  94.0 0.3 shard_map.126
  94.3 1.3 collective-permute-start.15
  95.6 1.4 collective-permute-start.17
  97.1 5.9 %collective-permute-done.19.other = bf16[512,128]{1,0:T(8,128)(2,1)S(1)} collective-permute-done((bf16[512,128]{1,0:T(8,128)(2,1)S(1)}, bf16[512,128]{1,0:T(8,128)(2,1)S(1)}, u32[]{:S(2)}, u32[]{:S(2)}) %collective-permute-start.19) | collective-permute-done | bytes 131104 | tf_op jit(solution)/shard_map/prefix/ppermute | solution.py:420
  103.0 0.5 collective-permute-start.12
  103.5 1.6 %collective-permute-start.27 = (bf16[512,128]{1,0:T(8,128)(2,1)S(1)}, bf16[512,128]{1,0:T(8,128)(2,1)S(1)}, u32[]{:S(2)}, u32[]{:S(2)}) collective-permute-start(bf16[512,128]{1,0:T(8,128)(2,1)S(1)} %prefix.6.refs_0_.own), channel_id=1, source_target_pairs={{0,128},{32,160},{64,192},{96,224},{128,0},{160,32},{192,64},{224,... | collective-permute-start | bytes 393224 | tf_op jit(solution)/shard_map/prefix/ppermute | solution.py:420
  105.1 3.0 %collective-permute-done.15.far_up = bf16[2048,128]{1,0:T(8,128)(2,1)S(1)} collective-permute-done((bf16[2048,128]{1,0:T(8,128)(2,1)S(1)}, bf16[2048,128]{1,0:T(8,128)(2,1)S(1)}, u32[]{:S(2)}, u32[]{:S(2)}) %collective-permute-start.15) | collective-permute-done | bytes 524320 | tf_op jit(solution)/shard_map/sum_x1/ppermute | solution.py:416
  108.2 0.4 shard_map.127
  108.5 0.4 shard_map.128
  108.9 5.3 %collective-permute-done.27.other = bf16[512,128]{1,0:T(8,128)(2,1)S(1)} collective-permute-done((bf16[512,128]{1,0:T(8,128)(2,1)S(1)}, bf16[512,128]{1,0:T(8,128)(2,1)S(1)}, u32[]{:S(2)}, u32[]{:S(2)}) %collective-permute-start.27) | collective-permute-done | bytes 131104 | tf_op jit(solution)/shard_map/prefix/ppermute | solution.py:420
  114.3 1.3 collective-permute-start.20
  115.7 1.4 collective-permute-start.21
  117.1 1.8 %collective-permute-done.28.other = bf16[512,128]{1,0:T(8,128)(2,1)S(1)} collective-permute-done((bf16[512,128]{1,0:T(8,128)(2,1)S(1)}, bf16[512,128]{1,0:T(8,128)(2,1)S(1)}, u32[]{:S(2)}, u32[]{:S(2)}) %collective-permute-start.28) | collective-permute-done | bytes 131104 | tf_op jit(solution)/shard_map/prefix/ppermute | solution.py:420
  119.0 2.5 %collective-permute-start.23 = (bf16[1024,256]{1,0:T(8,128)(2,1)S(1)}, bf16[1024,256]{1,0:T(8,128)(2,1)S(1)}, u32[]{:S(2)}, u32[]{:S(2)}) collective-permute-start(bf16[1024,256]{1,0:T(8,128)(2,1)S(1)} %get-tuple-element.60), channel_id=1, source_target_pairs={{0,6},{2,0},{4,2},{6,4},{1,7},{3,1},{5,3},{7,5},{8,14},{10,8},{12,... | collective-permute-start | bytes 1572872 | tf_op jit(solution)/shard_map/sum_x2/ppermute | solution.py:416
  121.5 0.3 collective-permute-start.29
  121.8 6.9 %collective-permute-done.20.up = bf16[1024,256]{1,0:T(8,128)(2,1)S(1)} collective-permute-done((bf16[1024,256]{1,0:T(8,128)(2,1)S(1)}, bf16[1024,256]{1,0:T(8,128)(2,1)S(1)}, u32[]{:S(2)}, u32[]{:S(2)}) %collective-permute-start.20) | collective-permute-done | bytes 524320 | tf_op jit(solution)/shard_map/sum_x2/ppermute | solution.py:416
  128.7 0.1 shard_map.132
  128.8 1.1 collective-permute-start.26
  130.0 10.0 %collective-permute-done.22.up = bf16[1024,256]{1,0:T(8,128)(2,1)S(1)} collective-permute-done((bf16[1024,256]{1,0:T(8,128)(2,1)S(1)}, bf16[1024,256]{1,0:T(8,128)(2,1)S(1)}, u32[]{:S(2)}, u32[]{:S(2)}) %collective-permute-start.22) | collective-permute-done | bytes 524320 | tf_op jit(solution)/shard_map/sum_x2/ppermute | solution.py:416
  139.9 0.1 shard_map.131
  140.1 1.1 collective-permute-start.25
  141.1 0.1 shard_map.130
  141.3 2.5 %collective-permute-start.24 = (bf16[512,256]{1,0:T(8,128)(2,1)S(1)}, bf16[512,256]{1,0:T(8,128)(2,1)S(1)}, u32[]{:S(2)}, u32[]{:S(2)}) collective-permute-start(bf16[512,256]{1,0:T(8,128)(2,1)S(1)} %shard_map.130), channel_id=1, source_target_pairs={{0,24},{8,0},{16,8},{24,16},{1,25},{9,1},{17,9},{25,17},{2,26},{10... | collective-permute-start | bytes 786440 | tf_op jit(solution)/shard_map/back/ppermute | solution.py:416
  143.9 0.7 slice_bitcast_fusion
  144.6 0.1 shard_map.129.refs_0_
  144.7 3.4 %collective-permute-done.25.refs_2_ = bf16[512,256]{1,0:T(8,128)(2,1)S(1)} collective-permute-done((bf16[512,256]{1,0:T(8,128)(2,1)S(1)}, bf16[512,256]{1,0:T(8,128)(2,1)S(1)}, u32[]{:S(2)}, u32[]{:S(2)}) %collective-permute-start.25) | collective-permute-done | bytes 262176 | tf_op jit(solution)/shard_map/back/ppermute | solution.py:416
  148.1 3.7 %collective-permute-done.24.refs_1_ = bf16[512,256]{1,0:T(8,128)(2,1)S(1)} collective-permute-done((bf16[512,256]{1,0:T(8,128)(2,1)S(1)}, bf16[512,256]{1,0:T(8,128)(2,1)S(1)}, u32[]{:S(2)}, u32[]{:S(2)}) %collective-permute-start.24) | collective-permute-done | bytes 262176 | tf_op jit(solution)/shard_map/back/ppermute | solution.py:416
  151.9 1.1 shard_map.133
  (37 shorter events, 0.5 us)
Async XLA Ops:
  2.6 22.8 %collective-permute-start = (bf16[256,1280]{1,0:T(8,128)(2,1)}, bf16[256,1280]{1,0:T(8,128)(2,1)S(1)}, u32[]{:S(2)}, u32[]{:S(2)}) collective-permute-start(bf16[256,1280]{1,0:T(8,128)(2,1)} %shard_map.121.refs_0_), channel_id=1, source_target_pairs={{0,224},{32,0},{64,32},{96,64},{128,96},{160,128},{192,160},{224,1... | collective-permute-start | bytes 1966088 | tf_op jit(solution)/shard_map/weights/ppermute | solution.py:416
  9.0 19.1 %collective-permute-start.1 = (bf16[256,1280]{1,0:T(8,128)(2,1)}, bf16[256,1280]{1,0:T(8,128)(2,1)S(1)}, u32[]{:S(2)}, u32[]{:S(2)}) collective-permute-start(bf16[256,1280]{1,0:T(8,128)(2,1)} %shard_map.121.refs_0_), channel_id=1, source_target_pairs={{0,32},{32,64},{64,96},{96,128},{128,160},{160,192},{192,224},{224... | collective-permute-start | bytes 1966088 | tf_op jit(solution)/shard_map/weights/ppermute | solution.py:416
  22.5 41.5 %copy-start = (bf16[256,1280]{1,0:T(8,128)(2,1)S(1)}, bf16[256,1280]{1,0:T(8,128)(2,1)}, u32[]{:S(2)}) copy-start(bf16[256,1280]{1,0:T(8,128)(2,1)} %shard_map.121.refs_0_) | copy-start | bytes 1966084
  22.5 41.5 %copy-start.1 = (bf16[512,1280]{1,0:T(8,128)(2,1)S(1)}, bf16[512,1280]{1,0:T(8,128)(2,1)}, u32[]{:S(2)}) copy-start(bf16[512,1280]{1,0:T(8,128)(2,1)} %get-tuple-element.32.refs_8_.refs_12_) | copy-start | bytes 3932164
  22.5 30.9 %collective-permute-start.6 = (bf16[512,1280]{1,0:T(8,128)(2,1)}, bf16[512,1280]{1,0:T(8,128)(2,1)S(1)}, u32[]{:S(2)}, u32[]{:S(2)}) collective-permute-start(bf16[512,1280]{1,0:T(8,128)(2,1)} %get-tuple-element.32.refs_8_.refs_12_), channel_id=1, source_target_pairs={{0,8},{8,16},{16,24},{24,0},{1,9},{9,17},{17,25},{25,1},{2,10},{10... | collective-permute-start | bytes 3932168 | tf_op jit(solution)/shard_map/grads/ppermute | solution.py:416
  23.9 29.6 %collective-permute-start.7 = (bf16[512,1280]{1,0:T(8,128)(2,1)}, bf16[512,1280]{1,0:T(8,128)(2,1)S(1)}, u32[]{:S(2)}, u32[]{:S(2)}) collective-permute-start(bf16[512,1280]{1,0:T(8,128)(2,1)} %get-tuple-element.32.refs_8_.refs_12_), channel_id=1, source_target_pairs={{0,24},{8,0},{16,8},{24,16},{1,25},{9,1},{17,9},{25,17},{2,26},{10... | collective-permute-start | bytes 3932168 | tf_op jit(solution)/shard_map/grads/ppermute | solution.py:416
  25.4 15.1 %collective-permute-start.2 = (bf16[256,1280]{1,0:T(8,128)(2,1)S(1)}, bf16[256,1280]{1,0:T(8,128)(2,1)S(1)}, u32[]{:S(2)}, u32[]{:S(2)}) collective-permute-start(bf16[256,1280]{1,0:T(8,128)(2,1)S(1)} %collective-permute-done.refs_1_), channel_id=1, source_target_pairs={{0,224},{32,0},{64,32},{96,64},{128,96},{160,128},{192,160},{224,1... | collective-permute-start | bytes 1966088 | tf_op jit(solution)/shard_map/weights/ppermute | solution.py:416
  28.1 15.8 %collective-permute-start.3 = (bf16[256,1280]{1,0:T(8,128)(2,1)S(1)}, bf16[256,1280]{1,0:T(8,128)(2,1)S(1)}, u32[]{:S(2)}, u32[]{:S(2)}) collective-permute-start(bf16[256,1280]{1,0:T(8,128)(2,1)S(1)} %collective-permute-done.1.refs_2_), channel_id=1, source_target_pairs={{0,32},{32,64},{64,96},{96,128},{128,160},{160,192},{192,224},{224... | collective-permute-start | bytes 1966088 | tf_op jit(solution)/shard_map/weights/ppermute | solution.py:416
  40.5 14.9 %collective-permute-start.4 = (bf16[256,1280]{1,0:T(8,128)(2,1)S(1)}, bf16[256,1280]{1,0:T(8,128)(2,1)S(1)}, u32[]{:S(2)}, u32[]{:S(2)}) collective-permute-start(bf16[256,1280]{1,0:T(8,128)(2,1)S(1)} %collective-permute-done.2.refs_3_), channel_id=1, source_target_pairs={{0,224},{32,0},{64,32},{96,64},{128,96},{160,128},{192,160},{224,1... | collective-permute-start | bytes 1966088 | tf_op jit(solution)/shard_map/weights/ppermute | solution.py:416
  43.9 14.6 %collective-permute-start.5 = (bf16[256,1280]{1,0:T(8,128)(2,1)S(1)}, bf16[256,1280]{1,0:T(8,128)(2,1)S(1)}, u32[]{:S(2)}, u32[]{:S(2)}) collective-permute-start(bf16[256,1280]{1,0:T(8,128)(2,1)S(1)} %collective-permute-done.3.refs_4_), channel_id=1, source_target_pairs={{0,32},{32,64},{64,96},{96,128},{128,160},{160,192},{192,224},{224... | collective-permute-start | bytes 1966088 | tf_op jit(solution)/shard_map/weights/ppermute | solution.py:416
  58.6 16.1 %collective-permute-start.10 = (bf16[256,1280]{1,0:T(8,128)(2,1)S(1)}, bf16[256,1280]{1,0:T(8,128)(2,1)S(1)}, u32[]{:S(2)}, u32[]{:S(2)}) collective-permute-start(bf16[256,1280]{1,0:T(8,128)(2,1)S(1)} %get-tuple-element.35), channel_id=1, source_target_pairs={{0,8},{8,16},{16,24},{24,0},{1,9},{9,17},{17,25},{25,1},{2,10},{10... | collective-permute-start | bytes 1966088 | tf_op jit(solution)/shard_map/grads_far/ppermute | solution.py:416
  58.7 16.0 %collective-permute-start.11 = (bf16[256,1280]{1,0:T(8,128)(2,1)S(1)}, bf16[256,1280]{1,0:T(8,128)(2,1)S(1)}, u32[]{:S(2)}, u32[]{:S(2)}) collective-permute-start(bf16[256,1280]{1,0:T(8,128)(2,1)S(1)} %get-tuple-element.36), channel_id=1, source_target_pairs={{0,24},{8,0},{16,8},{24,16},{1,25},{9,1},{17,9},{25,17},{2,26},{10... | collective-permute-start | bytes 1966088 | tf_op jit(solution)/shard_map/grads_far/ppermute | solution.py:416
  61.4 13.3 %collective-permute-start.8 = (bf16[128,1280]{1,0:T(8,128)(2,1)S(1)}, bf16[128,1280]{1,0:T(8,128)(2,1)S(1)}, u32[]{:S(2)}, u32[]{:S(2)}) collective-permute-start(bf16[128,1280]{1,0:T(8,128)(2,1)S(1)} %get-tuple-element.33), channel_id=1, source_target_pairs={{0,32},{32,64},{64,96},{96,128},{128,160},{160,192},{192,224},{224... | collective-permute-start | bytes 983048 | tf_op jit(solution)/shard_map/weights_far/ppermute | solution.py:416
  61.4 13.3 %collective-permute-start.9 = (bf16[128,1280]{1,0:T(8,128)(2,1)S(1)}, bf16[128,1280]{1,0:T(8,128)(2,1)S(1)}, u32[]{:S(2)}, u32[]{:S(2)}) collective-permute-start(bf16[128,1280]{1,0:T(8,128)(2,1)S(1)} %get-tuple-element.34), channel_id=1, source_target_pairs={{0,224},{32,0},{64,32},{96,64},{128,96},{160,128},{192,160},{224,1... | collective-permute-start | bytes 983048 | tf_op jit(solution)/shard_map/weights_far/ppermute | solution.py:416
  74.7 13.9 %copy-start.2 = (bf16[512,128]{1,0:T(8,128)(2,1)S(1)}, bf16[512,128]{1,0:T(8,128)(2,1)}, u32[]{:S(2)}) copy-start(bf16[512,128]{1,0:T(8,128)(2,1)} %get-tuple-element.56.own) | copy-start | bytes 393220
  83.1 10.9 %collective-permute-start.14 = (bf16[2048,256]{1,0:T(8,128)(2,1)S(1)}, bf16[2048,256]{1,0:T(8,128)(2,1)S(1)}, u32[]{:S(2)}, u32[]{:S(2)}) collective-permute-start(bf16[2048,256]{1,0:T(8,128)(2,1)S(1)} %get-tuple-element.51), channel_id=1, source_target_pairs={{0,1},{1,0},{2,3},{3,2},{4,5},{5,4},{6,7},{7,6},{8,9},{9,8},{10,11... | collective-permute-start | bytes 3145736 | tf_op jit(solution)/shard_map/sum_c/ppermute | solution.py:420
  88.0 15.5 %collective-permute-start.13 = (bf16[2048,256]{1,0:T(8,128)(2,1)S(1)}, bf16[2048,256]{1,0:T(8,128)(2,1)S(1)}, u32[]{:S(2)}, u32[]{:S(2)}) collective-permute-start(bf16[2048,256]{1,0:T(8,128)(2,1)S(1)} %get-tuple-element.49), channel_id=1, source_target_pairs={{0,1},{1,0},{2,3},{3,2},{4,5},{5,4},{6,7},{7,6},{8,9},{9,8},{10,11... | collective-permute-start | bytes 3145736 | tf_op jit(solution)/shard_map/sum_c/ppermute | solution.py:420
  88.1 17.0 %collective-permute-start.16 = (bf16[2048,256]{1,0:T(8,128)(2,1)S(1)}, bf16[2048,256]{1,0:T(8,128)(2,1)S(1)}, u32[]{:S(2)}, u32[]{:S(2)}) collective-permute-start(bf16[2048,256]{1,0:T(8,128)(2,1)S(1)} %get-tuple-element.54), channel_id=1, source_target_pairs={{0,1},{1,0},{2,3},{3,2},{4,5},{5,4},{6,7},{7,6},{8,9},{9,8},{10,11... | collective-permute-start | bytes 3145736 | tf_op jit(solution)/shard_map/sum_c/ppermute | solution.py:420
  88.6 5.1 %collective-permute-start.18 = (bf16[512,128]{1,0:T(8,128)(2,1)S(1)}, bf16[512,128]{1,0:T(8,128)(2,1)S(1)}, u32[]{:S(2)}, u32[]{:S(2)}) collective-permute-start(bf16[512,128]{1,0:T(8,128)(2,1)S(1)} %copy-done.2), channel_id=1, source_target_pairs={{0,32},{32,0},{64,96},{96,64},{128,160},{160,128},{192,224},{224,1... | collective-permute-start | bytes 393224 | tf_op jit(solution)/shard_map/prefix/ppermute | solution.py:420
  93.7 9.3 %collective-permute-start.19 = (bf16[512,128]{1,0:T(8,128)(2,1)S(1)}, bf16[512,128]{1,0:T(8,128)(2,1)S(1)}, u32[]{:S(2)}, u32[]{:S(2)}) collective-permute-start(bf16[512,128]{1,0:T(8,128)(2,1)S(1)} %prefix.5.own), channel_id=1, source_target_pairs={{0,64},{32,96},{64,0},{96,32},{128,192},{160,224},{192,128},{224,1... | collective-permute-start | bytes 393224 | tf_op jit(solution)/shard_map/prefix/ppermute | solution.py:420
  94.3 13.9 %collective-permute-start.15 = (bf16[2048,128]{1,0:T(8,128)(2,1)S(1)}, bf16[2048,128]{1,0:T(8,128)(2,1)S(1)}, u32[]{:S(2)}, u32[]{:S(2)}) collective-permute-start(bf16[2048,128]{1,0:T(8,128)(2,1)S(1)} %get-tuple-element.52), channel_id=1, source_target_pairs={{0,2},{2,4},{4,6},{6,0},{1,3},{3,5},{5,7},{7,1},{8,10},{10,12},{12... | collective-permute-start | bytes 1572872 | tf_op jit(solution)/shard_map/sum_x1/ppermute | solution.py:416
  95.6 12.5 %collective-permute-start.17 = (bf16[2048,128]{1,0:T(8,128)(2,1)S(1)}, bf16[2048,128]{1,0:T(8,128)(2,1)S(1)}, u32[]{:S(2)}, u32[]{:S(2)}) collective-permute-start(bf16[2048,128]{1,0:T(8,128)(2,1)S(1)} %get-tuple-element.55), channel_id=1, source_target_pairs={{0,6},{2,0},{4,2},{6,4},{1,7},{3,1},{5,3},{7,5},{8,14},{10,8},{12,... | collective-permute-start | bytes 1572872 | tf_op jit(solution)/shard_map/sum_x1/ppermute | solution.py:416
  103.0 18.5 %collective-permute-start.12 = (bf16[2048,256]{1,0:T(8,128)(2,1)S(1)}, bf16[2048,256]{1,0:T(8,128)(2,1)S(1)}, u32[]{:S(2)}, u32[]{:S(2)}) collective-permute-start(bf16[2048,256]{1,0:T(8,128)(2,1)S(1)} %get-tuple-element.47), channel_id=1, source_target_pairs={{0,1},{1,0},{2,3},{3,2},{4,5},{5,4},{6,7},{7,6},{8,9},{9,8},{10,11... | collective-permute-start | bytes 3145736 | tf_op jit(solution)/shard_map/sum_c/ppermute | solution.py:420
  103.5 10.7 %collective-permute-start.27 = (bf16[512,128]{1,0:T(8,128)(2,1)S(1)}, bf16[512,128]{1,0:T(8,128)(2,1)S(1)}, u32[]{:S(2)}, u32[]{:S(2)}) collective-permute-start(bf16[512,128]{1,0:T(8,128)(2,1)S(1)} %prefix.6.refs_0_.own), channel_id=1, source_target_pairs={{0,128},{32,160},{64,192},{96,224},{128,0},{160,32},{192,64},{224,... | collective-permute-start | bytes 393224 | tf_op jit(solution)/shard_map/prefix/ppermute | solution.py:420
  114.2 4.7 %collective-permute-start.28 = (bf16[512,128]{1,0:T(8,128)(2,1)S(1)}, bf16[512,128]{1,0:T(8,128)(2,1)S(1)}, u32[]{:S(2)}, u32[]{:S(2)}) collective-permute-start(bf16[512,128]{1,0:T(8,128)(2,1)S(1)} %prefix.7.own), channel_id=1, source_target_pairs={{0,8},{8,0},{16,24},{24,16},{1,9},{9,1},{17,25},{25,17},{2,10},{10... | collective-permute-start | bytes 393224 | tf_op jit(solution)/shard_map/prefix/ppermute | solution.py:420
  114.3 14.3 %collective-permute-start.20 = (bf16[1024,256]{1,0:T(8,128)(2,1)S(1)}, bf16[1024,256]{1,0:T(8,128)(2,1)S(1)}, u32[]{:S(2)}, u32[]{:S(2)}) collective-permute-start(bf16[1024,256]{1,0:T(8,128)(2,1)S(1)} %get-tuple-element.58.refs_0_), channel_id=1, source_target_pairs={{0,2},{2,4},{4,6},{6,0},{1,3},{3,5},{5,7},{7,1},{8,10},{10,12},{12... | collective-permute-start | bytes 1572872 | tf_op jit(solution)/shard_map/sum_x2/ppermute | solution.py:416
  115.7 13.0 %collective-permute-start.21 = (bf16[1024,256]{1,0:T(8,128)(2,1)S(1)}, bf16[1024,256]{1,0:T(8,128)(2,1)S(1)}, u32[]{:S(2)}, u32[]{:S(2)}) collective-permute-start(bf16[1024,256]{1,0:T(8,128)(2,1)S(1)} %get-tuple-element.59), channel_id=1, source_target_pairs={{0,6},{2,0},{4,2},{6,4},{1,7},{3,1},{5,3},{7,5},{8,14},{10,8},{12,... | collective-permute-start | bytes 1572872 | tf_op jit(solution)/shard_map/sum_x2/ppermute | solution.py:416
  117.1 22.8 %collective-permute-start.22 = (bf16[1024,256]{1,0:T(8,128)(2,1)S(1)}, bf16[1024,256]{1,0:T(8,128)(2,1)S(1)}, u32[]{:S(2)}, u32[]{:S(2)}) collective-permute-start(bf16[1024,256]{1,0:T(8,128)(2,1)S(1)} %get-tuple-element.57.refs_0_), channel_id=1, source_target_pairs={{0,2},{2,4},{4,6},{6,0},{1,3},{3,5},{5,7},{7,1},{8,10},{10,12},{12... | collective-permute-start | bytes 1572872 | tf_op jit(solution)/shard_map/sum_x2/ppermute | solution.py:416
  119.0 21.0 %collective-permute-start.23 = (bf16[1024,256]{1,0:T(8,128)(2,1)S(1)}, bf16[1024,256]{1,0:T(8,128)(2,1)S(1)}, u32[]{:S(2)}, u32[]{:S(2)}) collective-permute-start(bf16[1024,256]{1,0:T(8,128)(2,1)S(1)} %get-tuple-element.60), channel_id=1, source_target_pairs={{0,6},{2,0},{4,2},{6,4},{1,7},{3,1},{5,3},{7,5},{8,14},{10,8},{12,... | collective-permute-start | bytes 1572872 | tf_op jit(solution)/shard_map/sum_x2/ppermute | solution.py:416
  121.5 22.3 %collective-permute-start.29 = (bf16[512,128]{1,0:T(8,128)(2,1)S(1)}, bf16[512,128]{1,0:T(8,128)(2,1)S(1)}, u32[]{:S(2)}, u32[]{:S(2)}) collective-permute-start(bf16[512,128]{1,0:T(8,128)(2,1)S(1)} %prefix.8.own), channel_id=1, source_target_pairs={{0,16},{8,24},{16,0},{24,8},{1,17},{9,25},{17,1},{25,9},{2,18},{10... | collective-permute-start | bytes 393224 | tf_op jit(solution)/shard_map/prefix/ppermute | solution.py:420
  128.8 15.9 %collective-permute-start.26 = (bf16[512,256]{1,0:T(8,128)(2,1)S(1)}, bf16[512,256]{1,0:T(8,128)(2,1)S(1)}, u32[]{:S(2)}, u32[]{:S(2)}) collective-permute-start(bf16[512,256]{1,0:T(8,128)(2,1)S(1)} %shard_map.132), channel_id=1, source_target_pairs={{0,8},{8,16},{16,24},{24,0},{1,9},{9,17},{17,25},{25,1},{2,10},{10... | collective-permute-start | bytes 786440 | tf_op jit(solution)/shard_map/back/ppermute | solution.py:416
  140.1 8.1 %collective-permute-start.25 = (bf16[512,256]{1,0:T(8,128)(2,1)S(1)}, bf16[512,256]{1,0:T(8,128)(2,1)S(1)}, u32[]{:S(2)}, u32[]{:S(2)}) collective-permute-start(bf16[512,256]{1,0:T(8,128)(2,1)S(1)} %shard_map.131), channel_id=1, source_target_pairs={{0,16},{8,24},{16,0},{24,8},{1,17},{9,25},{17,1},{25,9},{2,18},{10... | collective-permute-start | bytes 786440 | tf_op jit(solution)/shard_map/back/ppermute | solution.py:416
  141.3 10.6 %collective-permute-start.24 = (bf16[512,256]{1,0:T(8,128)(2,1)S(1)}, bf16[512,256]{1,0:T(8,128)(2,1)S(1)}, u32[]{:S(2)}, u32[]{:S(2)}) collective-permute-start(bf16[512,256]{1,0:T(8,128)(2,1)S(1)} %shard_map.130), channel_id=1, source_target_pairs={{0,24},{8,0},{16,8},{24,16},{1,25},{9,1},{17,9},{25,17},{2,26},{10... | collective-permute-start | bytes 786440 | tf_op jit(solution)/shard_map/back/ppermute | solution.py:416
